TPU v7x, 256 devices: a whole 4x4x8 slice. The times are simulated.
256 devices in a mesh: pb: 64 (over z, x, core), ka: 4 (over y).
Axes of the slice: x: 4, y: 4, z: 8, core: 2. Of those that a mesh axis runs over, the one named last changes fastest.
Arguments:
- queries: bfloat16 [65536, 512], P('pb'), may hold values from -80 to 80
- key_cache: bfloat16 [65536, 128], P(('ka', 'pb')), may hold values from -4.1 to 4.1
- value_cache: bfloat16 [65536, 128], P(('ka', 'pb')), may hold values from -4 to 4
- block_list: int32 [512, 32], P('pb'), may hold values from 0 to 511, as said below
- block_count: int32 [512], P('pb'), may hold values from 1 to 32, as said below
Outputs:
- attended: bfloat16 [65536, 512], P(('pb', 'ka'))
Inputs may be any that keep to these rules, and one draw needn't show every extreme that they name: `block_list`: entries of row qb before block_count[qb] are distinct blocks at most qb, and qb itself is among them. They are the blocks v at most qb of one set of 16 vertical blocks, then the blocks qb - o at least 0 (and not already listed) of one set of 16 slash offsets; both sets contain 0 and lie below 128. Later entries equal qb. `block_count`: the number of distinct listed blocks of each query block.
All inputs are finite; a program needn't handle non-finite values.
Results may differ from a plain program's by a relative error of at most 0.0046.
Values may be sent and summed in bfloat16 or wider, within the bound.
A program may use at most 128 MiB of HBM per device.

v0:
```python
import math
import jax
import jax.numpy as jnp
from jax import lax
from jax.sharding import PartitionSpec as P

HD = 128
QH = 4
BLK = 128
LIST = 32
masked_score = -1e30


def merged(shard, axis, combine):
    everything = jax.tree.map(lambda part: lax.all_gather(part, axis), shard)
    initial = jax.tree.map(lambda part: part[0], everything)

    def lap(k, so_far):
        return combine(so_far, jax.tree.map(lambda part: part[k], everything))

    return lax.fori_loop(1, lax.axis_size(axis), lap, initial)


def combine(first, second):
    peak_first, sum_first, out_first = first
    peak_second, sum_second, out_second = second
    peak_both = jnp.maximum(peak_first, peak_second)
    factor_first = jnp.exp(peak_first - peak_both)
    factor_second = jnp.exp(peak_second - peak_both)
    sum_both = factor_first * sum_first + factor_second * sum_second
    out_both = (
        jnp.repeat(factor_first, HD, axis=1) * out_first
        + jnp.repeat(factor_second, HD, axis=1) * out_second
    )
    return (peak_both, sum_both, out_both)


def shards(queries, key_cache, value_cache, block_list, block_count):
    shard_keys, shard_values = (
        lax.all_gather(key_cache, "pb", axis=0, tiled=True),
        lax.all_gather(value_cache, "pb", axis=0, tiled=True),
    )
    group_index = lax.axis_index("pb")
    shard_index = lax.axis_index("ka")
    ka_width = lax.axis_size("ka")
    score_scale = 1.0 / math.sqrt(HD)
    shard_width = shard_keys.shape[0] // BLK
    local_blocks = queries.shape[0] // BLK
    first_block = shard_index * shard_width
    all_key_tiles = shard_keys.reshape(shard_width, BLK, HD)
    all_value_tiles = shard_values.reshape(shard_width, BLK, HD)
    slot_ids = jnp.arange(LIST, dtype=jnp.int32)
    position = jnp.arange(BLK, dtype=jnp.int32)

    def one_block(block_pos):
        query_rows = lax.dynamic_slice_in_dim(queries, block_pos * BLK, BLK, 0).reshape(BLK, QH, HD)
        listed = lax.dynamic_index_in_dim(block_list, block_pos, 0, keepdims=False)
        live_count = lax.dynamic_index_in_dim(block_count, block_pos, 0, keepdims=False)
        global_pos = group_index * local_blocks + block_pos
        live_slot = slot_ids < live_count
        local_ids = listed - first_block
        tile_live = live_slot & (local_ids >= 0) & (local_ids < shard_width)
        picked = jnp.clip(local_ids, 0, shard_width - 1)
        key_tiles = all_key_tiles[picked]
        value_tiles = all_value_tiles[picked]
        scores = (
            jnp.einsum("qhd,skd->hqsk", query_rows, key_tiles, preferred_element_type=jnp.float32)
            * score_scale
        )
        earlier = (listed < global_pos)[None, :, None]
        diagonal = (listed == global_pos)[None, :, None] & (
            position[None, None, :] <= position[:, None, None]
        )
        valid = tile_live[None, :, None] & (earlier | diagonal)
        masked = jnp.where(valid[None], scores, masked_score)
        peak_row = jnp.max(masked, axis=(2, 3))
        weights = jnp.where(valid[None], jnp.exp(scores - peak_row[..., None, None]), 0.0)
        weight_sum = jnp.sum(weights, axis=(2, 3))
        partial_out = jnp.einsum(
            "hqsk,skd->qhd",
            weights.astype(jnp.bfloat16),
            value_tiles,
            preferred_element_type=jnp.float32,
        )
        return (peak_row.T, weight_sum.T, partial_out.reshape(BLK, QH * HD))

    peaks, sums, outputs = lax.map(one_block, jnp.arange(local_blocks, dtype=jnp.int32))
    peaks = peaks.reshape(local_blocks * BLK, QH)
    sums = sums.reshape(local_blocks * BLK, QH)
    outputs = outputs.reshape(local_blocks * BLK, QH * HD)
    merged_peak, merged_sum, merged_out = merged((peaks, sums, outputs), "ka", combine)
    owned = merged_out.shape[0] // ka_width
    out_share = lax.dynamic_slice_in_dim(merged_out, shard_index * owned, owned, 0)
    sum_share = lax.dynamic_slice_in_dim(merged_sum, shard_index * owned, owned, 0)
    return (out_share / jnp.repeat(sum_share, HD, axis=1)).astype(jnp.bfloat16)


def solution(mesh):
    placed = (P("pb", None), P(("ka", "pb"), None), P(("ka", "pb"), None), P("pb", None), P("pb"))
    return jax.shard_map(
        shards, mesh=mesh, in_specs=placed, out_specs=P(("pb", "ka"), None), check_vma=False
    )
```

profile of v0, /device:TPU:1, one launch (start us, length us, event | category | flops | bytes accessed | tf_op | source)
XLA Modules:
  0.0 492.1 jit_solution(4541151159910000270)
XLA Ops:
  8.1 85.3 %all-gather.4.cloned.1.call-done = bf16[16384,128]{1,0:T(8,128)(2,1)} async-done(((bf16[256,128]{1,0:T(8,128)(2,1)}), bf16[16384,128]{1,0:T(8,128)(2,1)}) %all-gather.4.cloned.1.call-update) | async-done | bytes 4194320 | tf_op jit(solution)/shard_map/all_gather | solution.py:40
  93.3 79.1 %all-gather.6.cloned.1.call-done = bf16[16384,128]{1,0:T(8,128)(2,1)} async-done(((bf16[256,128]{1,0:T(8,128)(2,1)}), bf16[16384,128]{1,0:T(8,128)(2,1)}) %all-gather.6.cloned.1.call-update) | async-done | bytes 4194320 | tf_op jit(solution)/shard_map/all_gather | solution.py:41
  172.4 201.8 %while.37 = (s32[]{:T(128)}, f32[8,128,4]{1,2,0:T(4,128)S(1)}, f32[8,128,4]{1,2,0:T(4,128)S(1)}, f32[8,128,512]{2,1,0:T(8,128)}, s32[8]{0:T(128)S(1)}, /*index=5...) while((s32[]{:T(128)}, f32[8,128,4]{1,2,0:T(4,128)S(1)}, ...), condition=%wide.region_3.4_spmd.clone, body=%wide.region_0.3_spmd.clone.sunk | while | flops 1098400256 | bytes 69129872 | solution.py:87
  181.2 2.9 gather_fusion
  185.4 1.9 fusion.40
  187.3 1.3 copy-done
  188.6 2.9 gather_fusion.1
  191.6 5.2 %fusion.41 = f32[128,4,128,1]{2,0,1,3:T(8,128)S(1)} fusion(f32[32,128,128,4]{2,1,3,0:T(8,128)} %copy-done, f32[4,128]{1,0:T(4,128)S(1)} %get-tuple-element.581, pred[128,32,128]{0,2,1:T(8,128)(4,1)S(1)} %or_and_fusion.2, bf16[32,128,128]{2,1,0:T(8,128)(2,1)S(1)} %gather_fusion.1), kind=kOutput, calls=%fused_computation.20.clone.1 | convolution fusion | flops 545259520 | bytes 10225664 | tf_op jit(solution)/shard_map/while/body/eval_jaxpr/hqsk,skd->qhd/dot_general | solution.py:79
  206.4 2.9 gather_fusion
  210.6 1.9 fusion.40
  212.5 1.3 copy-done
  213.9 2.9 gather_fusion.1
  216.8 5.2 %fusion.41 = f32[128,4,128,1]{2,0,1,3:T(8,128)S(1)} fusion(f32[32,128,128,4]{2,1,3,0:T(8,128)} %copy-done, f32[4,128]{1,0:T(4,128)S(1)} %get-tuple-element.581, pred[128,32,128]{0,2,1:T(8,128)(4,1)S(1)} %or_and_fusion.2, bf16[32,128,128]{2,1,0:T(8,128)(2,1)S(1)} %gather_fusion.1), kind=kOutput, calls=%fused_computation.20.clone.1 | convolution fusion | flops 545259520 | bytes 10225664 | tf_op jit(solution)/shard_map/while/body/eval_jaxpr/hqsk,skd->qhd/dot_general | solution.py:79
  231.7 2.9 gather_fusion
  235.9 1.9 fusion.40
  237.7 1.3 copy-done
  239.1 2.9 gather_fusion.1
  242.0 5.2 %fusion.41 = f32[128,4,128,1]{2,0,1,3:T(8,128)S(1)} fusion(f32[32,128,128,4]{2,1,3,0:T(8,128)} %copy-done, f32[4,128]{1,0:T(4,128)S(1)} %get-tuple-element.581, pred[128,32,128]{0,2,1:T(8,128)(4,1)S(1)} %or_and_fusion.2, bf16[32,128,128]{2,1,0:T(8,128)(2,1)S(1)} %gather_fusion.1), kind=kOutput, calls=%fused_computation.20.clone.1 | convolution fusion | flops 545259520 | bytes 10225664 | tf_op jit(solution)/shard_map/while/body/eval_jaxpr/hqsk,skd->qhd/dot_general | solution.py:79
  256.9 2.9 gather_fusion
  261.1 1.9 fusion.40
  262.9 1.3 copy-done
  264.3 2.9 gather_fusion.1
  267.2 5.2 %fusion.41 = f32[128,4,128,1]{2,0,1,3:T(8,128)S(1)} fusion(f32[32,128,128,4]{2,1,3,0:T(8,128)} %copy-done, f32[4,128]{1,0:T(4,128)S(1)} %get-tuple-element.581, pred[128,32,128]{0,2,1:T(8,128)(4,1)S(1)} %or_and_fusion.2, bf16[32,128,128]{2,1,0:T(8,128)(2,1)S(1)} %gather_fusion.1), kind=kOutput, calls=%fused_computation.20.clone.1 | convolution fusion | flops 545259520 | bytes 10225664 | tf_op jit(solution)/shard_map/while/body/eval_jaxpr/hqsk,skd->qhd/dot_general | solution.py:79
  282.1 2.9 gather_fusion
  286.3 1.9 fusion.40
  289.5 2.9 gather_fusion.1
  292.4 5.2 %fusion.41 = f32[128,4,128,1]{2,0,1,3:T(8,128)S(1)} fusion(f32[32,128,128,4]{2,1,3,0:T(8,128)} %copy-done, f32[4,128]{1,0:T(4,128)S(1)} %get-tuple-element.581, pred[128,32,128]{0,2,1:T(8,128)(4,1)S(1)} %or_and_fusion.2, bf16[32,128,128]{2,1,0:T(8,128)(2,1)S(1)} %gather_fusion.1), kind=kOutput, calls=%fused_computation.20.clone.1 | convolution fusion | flops 545259520 | bytes 10225664 | tf_op jit(solution)/shard_map/while/body/eval_jaxpr/hqsk,skd->qhd/dot_general | solution.py:79
  307.3 2.9 gather_fusion
  311.5 1.9 fusion.40
  314.7 2.9 gather_fusion.1
  317.7 5.2 %fusion.41 = f32[128,4,128,1]{2,0,1,3:T(8,128)S(1)} fusion(f32[32,128,128,4]{2,1,3,0:T(8,128)} %copy-done, f32[4,128]{1,0:T(4,128)S(1)} %get-tuple-element.581, pred[128,32,128]{0,2,1:T(8,128)(4,1)S(1)} %or_and_fusion.2, bf16[32,128,128]{2,1,0:T(8,128)(2,1)S(1)} %gather_fusion.1), kind=kOutput, calls=%fused_computation.20.clone.1 | convolution fusion | flops 545259520 | bytes 10225664 | tf_op jit(solution)/shard_map/while/body/eval_jaxpr/hqsk,skd->qhd/dot_general | solution.py:79
  332.5 2.9 gather_fusion
  336.7 1.9 fusion.40
  339.9 2.9 gather_fusion.1
  342.9 5.2 %fusion.41 = f32[128,4,128,1]{2,0,1,3:T(8,128)S(1)} fusion(f32[32,128,128,4]{2,1,3,0:T(8,128)} %copy-done, f32[4,128]{1,0:T(4,128)S(1)} %get-tuple-element.581, pred[128,32,128]{0,2,1:T(8,128)(4,1)S(1)} %or_and_fusion.2, bf16[32,128,128]{2,1,0:T(8,128)(2,1)S(1)} %gather_fusion.1), kind=kOutput, calls=%fused_computation.20.clone.1 | convolution fusion | flops 545259520 | bytes 10225664 | tf_op jit(solution)/shard_map/while/body/eval_jaxpr/hqsk,skd->qhd/dot_general | solution.py:79
  357.7 2.9 gather_fusion
  361.9 1.9 fusion.40
  365.2 2.9 gather_fusion.1
  368.1 5.2 %fusion.41 = f32[128,4,128,1]{2,0,1,3:T(8,128)S(1)} fusion(f32[32,128,128,4]{2,1,3,0:T(8,128)} %copy-done, f32[4,128]{1,0:T(4,128)S(1)} %get-tuple-element.581, pred[128,32,128]{0,2,1:T(8,128)(4,1)S(1)} %or_and_fusion.2, bf16[32,128,128]{2,1,0:T(8,128)(2,1)S(1)} %gather_fusion.1), kind=kOutput, calls=%fused_computation.20.clone.1 | convolution fusion | flops 545259520 | bytes 10225664 | tf_op jit(solution)/shard_map/while/body/eval_jaxpr/hqsk,skd->qhd/dot_general | solution.py:79
  374.2 9.6 %all_gather.17 = f32[4,1024,4]{1,2,0:T(4,128)S(1)} all-gather(f32[1,1024,4]{1,2,0:T(4,128)S(1)} %bitcast.155), channel_id=1, replica_groups=mesh['pb'=64,'ka'=4] {'ka'}, dimensions={0}, use_global_device_ids=true | all-gather | bytes 81920 | tf_op jit(solution)/shard_map/all_gather | solution.py:15
  383.8 9.9 %all_gather.18 = f32[4,1024,4]{1,2,0:T(4,128)S(1)} all-gather(f32[1,1024,4]{1,2,0:T(4,128)S(1)} %bitcast.156), channel_id=1, replica_groups=mesh['pb'=64,'ka'=4] {'ka'}, dimensions={0}, use_global_device_ids=true | all-gather | bytes 81920 | tf_op jit(solution)/shard_map/all_gather | solution.py:15
  393.7 63.6 %all-gather.8.cloned.1.call-done = f32[4,1024,512]{2,1,0:T(8,128)} async-done(((f32[1,1024,512]{2,1,0:T(8,128)}), f32[4,1024,512]{2,1,0:T(8,128)}) %all-gather.8.cloned.1.call-update) | async-done | bytes 8388624 | tf_op jit(solution)/shard_map/all_gather | solution.py:15
  457.3 3.1 slice_bitcast_fusion
  460.5 22.8 %while.36 = (s32[]{:T(128)}, f32[1024,4]{0,1:T(4,128)S(1)}, f32[1024,4]{0,1:T(4,128)S(1)}, f32[1024,512]{1,0:T(8,128)}, f32[4,1024,4]{1,2,0:T(4,128)S(1)}, /*ind...) while((s32[]{:T(128)}, f32[1024,4]{0,1:T(4,128)S(1)}, ...), condition=%wide.region_5.6_spmd, body=%wide.region_4.5_spmd.sunk | while | flops 1597445 | bytes 14909591 | solution.py:21
  463.4 4.6 fusion.34
  471.0 4.6 fusion.34
  478.6 4.6 fusion.34
  483.7 1.8 fusion.21
  (162 shorter events, 77.6 us)
Async XLA Ops:
  6.5 86.8 %all-gather.4.cloned.1.call-start = ((), (), s32[]{:S(2)}) async-start(), calls=%async_computation | async-start | bytes 4259840 | tf_op jit(solution)/shard_map/all_gather | solution.py:40
  7.3 165.1 %all-gather.6.cloned.1.call-start = ((), (), s32[]{:S(2)}) async-start(), calls=%async_computation.1 | async-start | bytes 4259840 | tf_op jit(solution)/shard_map/all_gather | solution.py:41
  8.0 449.3 %all-gather.8.cloned.1.call-start = ((), (), s32[]{:S(2)}) async-start(), calls=%async_computation.2 | async-start | bytes 10485760 | tf_op jit(solution)/shard_map/all_gather | solution.py:15
  185.4 3.2 copy-start
  210.6 3.2 copy-start
  235.8 3.2 copy-start
  261.1 3.2 copy-start
  286.3 3.2 copy-start
  311.5 3.2 copy-start
  336.7 3.2 copy-start
  361.9 3.2 copy-start
Sparse Core Ops, SparseCore 0:
  10.1 83.1 all-gather.3
  96.1 76.2 all-gather.5
  374.3 82.9 all-gather.7
where the time goes:
time: 494 us; the launch traced here: 492 us
  waiting for transfers between devices  229 us (46%)
  local copies, waits for them, and re-layouts  101 us (20%)
  other arithmetic  51.8 us (10%)
  matrix products  51.4 us (10%)
  loops' own time  26.3 us (5%)
  blocking collectives  19.5 us (4%)
  between operations  13.1 us (3%)
    all_gather x1, waiting for transfers between devices, shards(): lax.all_gather(key_cache, 'pb', axis=0, tiled=True)  85.3 us
    all_gather x1, waiting for transfers between devices, shards(): lax.all_gather(value_cache, 'pb', axis=0, tiled=True)  79.1 us
    all_gather x1, waiting for transfers between devices, merged(): everything = jax.tree.map(lambda part: lax.all_gather(part, axis), shard)  63.6 us
    dot_general x8, matrix products, one_block(): jnp.einsum('hqsk,skd->qhd', weights.astype(jnp.bfloat16), value_tiles, pr...  41.5 us
    another operation x1, loops' own time, shards(): lax.map(one_block, jnp.arange(local_blocks, dtype=jnp.int32))  26.2 us
    gather x8, local copies, waits for them, and re-layouts, one_block(): key_tiles = all_key_tiles[picked]  23.5 us
    gather x8, local copies, waits for them, and re-layouts, one_block(): value_tiles = all_value_tiles[picked]  23.5 us
    all_gather x2, blocking collectives, merged(): everything = jax.tree.map(lambda part: lax.all_gather(part, axis), shard)  19.5 us
  transfers between devices with their start and end apart: 3, of which 3 were waited for; matrix products, arithmetic and copies ran while one was open for 0% of the time, Pallas kernels for 0%

commit v1 on v0

--- a/solution.py
+++ b/solution.py
@@ -9,6 +9,14 @@
 BLK = 128
 LIST = 32
 masked_score = -1e30
+
+
+def gather_by_exchange(shard, axis, dim):
+    size = lax.axis_size(axis)
+    repeats = [size if d == dim else 1 for d in range(shard.ndim)]
+    return lax.all_to_all(
+        jnp.tile(shard, repeats), axis, split_axis=dim, concat_axis=dim, tiled=True
+    )
 
 
 def merged(shard, axis, combine):
@@ -38,7 +46,7 @@
 def shards(queries, key_cache, value_cache, block_list, block_count):
     shard_keys, shard_values = (
         lax.all_gather(key_cache, "pb", axis=0, tiled=True),
-        lax.all_gather(value_cache, "pb", axis=0, tiled=True),
+        gather_by_exchange(value_cache, "pb", 0),
     )
     group_index = lax.axis_index("pb")
     shard_index = lax.axis_index("ka")

time: 494 us -> 449 us (0.909)
  waiting for transfers between devices: 229 us -> 173 us
  starting transfers between devices: 0.08 us -> 13.4 us
    all_gather x1 -> x0, waiting for transfers between devices: 79.1 us -> none  [shards(): lax.all_gather(value_cache, 'pb', axis=0, tiled=True)]
    all_to_all x0 -> x1, waiting for transfers between devices: none -> 16.6 us  [gather_by_exchange(): lax.all_to_all(jnp.tile(shard, repeats), axis, split_axis=dim, concat_axi...]
    all_to_all x0 -> x1, starting transfers between devices: none -> 13.3 us  [gather_by_exchange(): lax.all_to_all(jnp.tile(shard, repeats), axis, split_axis=dim, concat_axi...]
    dynamic_slice x8, local copies, waits for them, and re-layouts: 10.5 us -> 5.22 us  [one_block(): lax.dynamic_index_in_dim(block_count, block_pos, 0, keepdims=False)]
  transfers between devices with their start and end apart: 3 -> 3, of which waited for: 3 -> 3; matrix products, arithmetic and copies ran while one was open for 0% -> 1% of each run, Pallas kernels for 0% -> 0%
where the time goes in v1:
time: 449 us; the launch traced here: 447 us
  waiting for transfers between devices  173 us (39%)
  local copies, waits for them, and re-layouts  99.1 us (22%)
  other arithmetic  51.8 us (12%)
  matrix products  51.4 us (11%)
  loops' own time  26.3 us (6%)
  blocking collectives  19 us (4%)
  between operations  13.5 us (3%)
  starting transfers between devices  13.4 us (3%)
    all_gather x1, waiting for transfers between devices, shards(): lax.all_gather(key_cache, 'pb', axis=0, tiled=True)  90.1 us
    all_gather x1, waiting for transfers between devices, merged(): everything = jax.tree.map(lambda part: lax.all_gather(part, axis), shard)  65.2 us
    dot_general x8, matrix products, one_block(): jnp.einsum('hqsk,skd->qhd', weights.astype(jnp.bfloat16), value_tiles, pr...  41.5 us
    another operation x1, loops' own time, shards(): lax.map(one_block, jnp.arange(local_blocks, dtype=jnp.int32))  26.2 us
    gather x8, local copies, waits for them, and re-layouts, one_block(): key_tiles = all_key_tiles[picked]  23.5 us
    gather x8, local copies, waits for them, and re-layouts, one_block(): value_tiles = all_value_tiles[picked]  23.5 us
    all_gather x2, blocking collectives, merged(): everything = jax.tree.map(lambda part: lax.all_gather(part, axis), shard)  19 us
    all_to_all x1, waiting for transfers between devices, gather_by_exchange(): lax.all_to_all(jnp.tile(shard, repeats), axis, split_axis=dim, concat_axi...  16.6 us
  transfers between devices with their start and end apart: 3, of which 3 were waited for; matrix products, arithmetic and copies ran while one was open for 1% of the time, Pallas kernels for 0%

profile of v1, /device:TPU:1, one launch (start us, length us, event | category | flops | bytes accessed | tf_op | source)
XLA Modules:
  0.0 446.9 jit_solution(2412707682118810137)
XLA Ops:
  7.3 3.8 tile.2
  11.1 13.3 %all-to-all-start = ((bf16[64,256,128]{2,1,0:T(8,128)(2,1)}), bf16[64,256,128]{2,1,0:T(8,128)(2,1)}, u32[]{:S(2)}, u32[]{:S(2)}) async-start(bf16[64,256,128]{2,1,0:T(8,128)(2,1)} %tile.2), calls=%async_computation | async-start | bytes 8388608 | tf_op jit(solution)/shard_map/all_to_all | solution.py:17
  24.5 90.1 %all-gather.3.cloned.1.call-done = bf16[16384,128]{1,0:T(8,128)(2,1)} async-done(((bf16[256,128]{1,0:T(8,128)(2,1)}), bf16[16384,128]{1,0:T(8,128)(2,1)}) %all-gather.3.cloned.1.call-update) | async-done | bytes 4194320 | tf_op jit(solution)/shard_map/all_gather | solution.py:48
  114.5 16.6 %all-to-all-done = bf16[64,256,128]{2,1,0:T(8,128)(2,1)} async-done(((bf16[64,256,128]{2,1,0:T(8,128)(2,1)}), bf16[64,256,128]{2,1,0:T(8,128)(2,1)}, u32[]{:S(2)}, u32[]{:S(2)}) %all-to-all-start) | async-done | bytes 4194336 | tf_op jit(solution)/shard_map/all_to_all | solution.py:17
  131.1 196.5 %while.37 = (s32[]{:T(128)}, f32[8,128,4]{1,2,0:T(4,128)S(1)}, f32[8,128,4]{1,2,0:T(4,128)S(1)}, f32[8,128,512]{2,1,0:T(8,128)}, s32[8]{0:T(128)S(1)}, /*index=5...) while((s32[]{:T(128)}, f32[8,128,4]{1,2,0:T(4,128)S(1)}, ...), condition=%wide.region_3.4_spmd.clone, body=%wide.region_0.3_spmd.clone.sunk | while | flops 1098400256 | bytes 69129872 | solution.py:95
  139.2 2.9 gather_fusion
  143.4 1.9 fusion.40
  145.3 1.3 copy-done
  146.7 2.9 gather_fusion.1
  149.6 5.2 %fusion.41 = f32[128,4,128,1]{2,0,1,3:T(8,128)S(1)} fusion(f32[32,128,128,4]{2,1,3,0:T(8,128)} %copy-done, f32[4,128]{1,0:T(4,128)S(1)} %get-tuple-element.581, pred[128,32,128]{0,2,1:T(8,128)(4,1)S(1)} %or_and_fusion.2, bf16[32,128,128]{2,1,0:T(8,128)(2,1)S(1)} %gather_fusion.1), kind=kOutput, calls=%fused_computation.20.clone.1 | convolution fusion | flops 545259520 | bytes 10225664 | tf_op jit(solution)/shard_map/while/body/eval_jaxpr/hqsk,skd->qhd/dot_general | solution.py:87
  163.8 2.9 gather_fusion
  168.0 1.9 fusion.40
  169.9 1.3 copy-done
  171.2 2.9 gather_fusion.1
  174.2 5.2 %fusion.41 = f32[128,4,128,1]{2,0,1,3:T(8,128)S(1)} fusion(f32[32,128,128,4]{2,1,3,0:T(8,128)} %copy-done, f32[4,128]{1,0:T(4,128)S(1)} %get-tuple-element.581, pred[128,32,128]{0,2,1:T(8,128)(4,1)S(1)} %or_and_fusion.2, bf16[32,128,128]{2,1,0:T(8,128)(2,1)S(1)} %gather_fusion.1), kind=kOutput, calls=%fused_computation.20.clone.1 | convolution fusion | flops 545259520 | bytes 10225664 | tf_op jit(solution)/shard_map/while/body/eval_jaxpr/hqsk,skd->qhd/dot_general | solution.py:87
  188.4 2.9 gather_fusion
  192.6 1.9 fusion.40
  195.8 2.9 gather_fusion.1
  198.7 5.2 %fusion.41 = f32[128,4,128,1]{2,0,1,3:T(8,128)S(1)} fusion(f32[32,128,128,4]{2,1,3,0:T(8,128)} %copy-done, f32[4,128]{1,0:T(4,128)S(1)} %get-tuple-element.581, pred[128,32,128]{0,2,1:T(8,128)(4,1)S(1)} %or_and_fusion.2, bf16[32,128,128]{2,1,0:T(8,128)(2,1)S(1)} %gather_fusion.1), kind=kOutput, calls=%fused_computation.20.clone.1 | convolution fusion | flops 545259520 | bytes 10225664 | tf_op jit(solution)/shard_map/while/body/eval_jaxpr/hqsk,skd->qhd/dot_general | solution.py:87
  212.9 2.9 gather_fusion
  217.1 1.9 fusion.40
  220.4 2.9 gather_fusion.1
  223.3 5.2 %fusion.41 = f32[128,4,128,1]{2,0,1,3:T(8,128)S(1)} fusion(f32[32,128,128,4]{2,1,3,0:T(8,128)} %copy-done, f32[4,128]{1,0:T(4,128)S(1)} %get-tuple-element.581, pred[128,32,128]{0,2,1:T(8,128)(4,1)S(1)} %or_and_fusion.2, bf16[32,128,128]{2,1,0:T(8,128)(2,1)S(1)} %gather_fusion.1), kind=kOutput, calls=%fused_computation.20.clone.1 | convolution fusion | flops 545259520 | bytes 10225664 | tf_op jit(solution)/shard_map/while/body/eval_jaxpr/hqsk,skd->qhd/dot_general | solution.py:87
  237.5 2.9 gather_fusion
  241.7 1.9 fusion.40
  244.9 2.9 gather_fusion.1
  247.8 5.2 %fusion.41 = f32[128,4,128,1]{2,0,1,3:T(8,128)S(1)} fusion(f32[32,128,128,4]{2,1,3,0:T(8,128)} %copy-done, f32[4,128]{1,0:T(4,128)S(1)} %get-tuple-element.581, pred[128,32,128]{0,2,1:T(8,128)(4,1)S(1)} %or_and_fusion.2, bf16[32,128,128]{2,1,0:T(8,128)(2,1)S(1)} %gather_fusion.1), kind=kOutput, calls=%fused_computation.20.clone.1 | convolution fusion | flops 545259520 | bytes 10225664 | tf_op jit(solution)/shard_map/while/body/eval_jaxpr/hqsk,skd->qhd/dot_general | solution.py:87
  262.1 2.9 gather_fusion
  266.3 1.9 fusion.40
  269.5 2.9 gather_fusion.1
  272.4 5.2 %fusion.41 = f32[128,4,128,1]{2,0,1,3:T(8,128)S(1)} fusion(f32[32,128,128,4]{2,1,3,0:T(8,128)} %copy-done, f32[4,128]{1,0:T(4,128)S(1)} %get-tuple-element.581, pred[128,32,128]{0,2,1:T(8,128)(4,1)S(1)} %or_and_fusion.2, bf16[32,128,128]{2,1,0:T(8,128)(2,1)S(1)} %gather_fusion.1), kind=kOutput, calls=%fused_computation.20.clone.1 | convolution fusion | flops 545259520 | bytes 10225664 | tf_op jit(solution)/shard_map/while/body/eval_jaxpr/hqsk,skd->qhd/dot_general | solution.py:87
  286.6 2.9 gather_fusion
  290.8 1.9 fusion.40
  294.1 2.9 gather_fusion.1
  297.0 5.2 %fusion.41 = f32[128,4,128,1]{2,0,1,3:T(8,128)S(1)} fusion(f32[32,128,128,4]{2,1,3,0:T(8,128)} %copy-done, f32[4,128]{1,0:T(4,128)S(1)} %get-tuple-element.581, pred[128,32,128]{0,2,1:T(8,128)(4,1)S(1)} %or_and_fusion.2, bf16[32,128,128]{2,1,0:T(8,128)(2,1)S(1)} %gather_fusion.1), kind=kOutput, calls=%fused_computation.20.clone.1 | convolution fusion | flops 545259520 | bytes 10225664 | tf_op jit(solution)/shard_map/while/body/eval_jaxpr/hqsk,skd->qhd/dot_general | solution.py:87
  311.2 2.9 gather_fusion
  315.4 1.9 fusion.40
  318.6 2.9 gather_fusion.1
  321.6 5.2 %fusion.41 = f32[128,4,128,1]{2,0,1,3:T(8,128)S(1)} fusion(f32[32,128,128,4]{2,1,3,0:T(8,128)} %copy-done, f32[4,128]{1,0:T(4,128)S(1)} %get-tuple-element.581, pred[128,32,128]{0,2,1:T(8,128)(4,1)S(1)} %or_and_fusion.2, bf16[32,128,128]{2,1,0:T(8,128)(2,1)S(1)} %gather_fusion.1), kind=kOutput, calls=%fused_computation.20.clone.1 | convolution fusion | flops 545259520 | bytes 10225664 | tf_op jit(solution)/shard_map/while/body/eval_jaxpr/hqsk,skd->qhd/dot_general | solution.py:87
  327.6 9.5 %all_gather.13 = f32[4,1024,4]{1,2,0:T(4,128)S(1)} all-gather(f32[1,1024,4]{1,2,0:T(4,128)S(1)} %bitcast.154), channel_id=1, replica_groups=mesh['pb'=64,'ka'=4] {'ka'}, dimensions={0}, use_global_device_ids=true | all-gather | bytes 81920 | tf_op jit(solution)/shard_map/all_gather | solution.py:23
  337.1 9.5 %all_gather.14 = f32[4,1024,4]{1,2,0:T(4,128)S(1)} all-gather(f32[1,1024,4]{1,2,0:T(4,128)S(1)} %bitcast.155), channel_id=1, replica_groups=mesh['pb'=64,'ka'=4] {'ka'}, dimensions={0}, use_global_device_ids=true | all-gather | bytes 81920 | tf_op jit(solution)/shard_map/all_gather | solution.py:23
  346.7 65.2 %all-gather.5.cloned.1.call-done = f32[4,1024,512]{2,1,0:T(8,128)} async-done(((f32[1,1024,512]{2,1,0:T(8,128)}), f32[4,1024,512]{2,1,0:T(8,128)}) %all-gather.5.cloned.1.call-update) | async-done | bytes 8388624 | tf_op jit(solution)/shard_map/all_gather | solution.py:23
  411.9 3.1 slice_bitcast_fusion
  415.0 22.8 %while.36 = (s32[]{:T(128)}, f32[1024,4]{0,1:T(4,128)S(1)}, f32[1024,4]{0,1:T(4,128)S(1)}, f32[1024,512]{1,0:T(8,128)}, f32[4,1024,4]{1,2,0:T(4,128)S(1)}, /*ind...) while((s32[]{:T(128)}, f32[1024,4]{0,1:T(4,128)S(1)}, ...), condition=%wide.region_5.6_spmd, body=%wide.region_4.5_spmd.sunk | while | flops 1597445 | bytes 14909591 | solution.py:29
  418.0 4.6 %fusion.34 = f32[1024,512]{1,0:T(8,128)} fusion(f32[128,8,4,128]{3,2,1,0:T(4,128)S(1)} %bitcast.147, f32[1024,512]{1,0:T(8,128)} %get-tuple-element.648, f32[128,8,4,128]{3,2,1,0:T(4,128)S(1)} %bitcast.148, f32[4,1024,512]{2,1,0:T(8,128)} %get-tuple-element.661, s32[]{:T(128)S(6)} %select_n.78), kind=kLoop, calls=%fused_computation.5.clone.1 | loop fusion | flops 1572864 | bytes 10485764 | tf_op jit(solution)/shard_map/while/body/eval_jaxpr/add | solution.py:40
  425.5 4.6 %fusion.34 = f32[1024,512]{1,0:T(8,128)} fusion(f32[128,8,4,128]{3,2,1,0:T(4,128)S(1)} %bitcast.147, f32[1024,512]{1,0:T(8,128)} %get-tuple-element.648, f32[128,8,4,128]{3,2,1,0:T(4,128)S(1)} %bitcast.148, f32[4,1024,512]{2,1,0:T(8,128)} %get-tuple-element.661, s32[]{:T(128)S(6)} %select_n.78), kind=kLoop, calls=%fused_computation.5.clone.1 | loop fusion | flops 1572864 | bytes 10485764 | tf_op jit(solution)/shard_map/while/body/eval_jaxpr/add | solution.py:40
  433.1 4.6 %fusion.34 = f32[1024,512]{1,0:T(8,128)} fusion(f32[128,8,4,128]{3,2,1,0:T(4,128)S(1)} %bitcast.147, f32[1024,512]{1,0:T(8,128)} %get-tuple-element.648, f32[128,8,4,128]{3,2,1,0:T(4,128)S(1)} %bitcast.148, f32[4,1024,512]{2,1,0:T(8,128)} %get-tuple-element.661, s32[]{:T(128)S(6)} %select_n.78), kind=kLoop, calls=%fused_computation.5.clone.1 | loop fusion | flops 1572864 | bytes 10485764 | tf_op jit(solution)/shard_map/while/body/eval_jaxpr/add | solution.py:40
  438.2 1.8 fusion.21
  (164 shorter events, 74.3 us)
Async XLA Ops:
  6.5 108.0 %all-gather.3.cloned.1.call-start = ((), (), s32[]{:S(2)}) async-start(), calls=%async_computation.1 | async-start | bytes 4259840 | tf_op jit(solution)/shard_map/all_gather | solution.py:48
  11.1 120.0 %copy-start.1 = (s32[8]{0:T(128)S(1)}, s32[8]{0:T(128)}, u32[]{:S(2)}) copy-start(s32[8]{0:T(128)} %param.13) | copy-start | bytes 100
  11.1 120.0 %all-to-all-start = ((bf16[64,256,128]{2,1,0:T(8,128)(2,1)}), bf16[64,256,128]{2,1,0:T(8,128)(2,1)}, u32[]{:S(2)}, u32[]{:S(2)}) async-start(bf16[64,256,128]{2,1,0:T(8,128)(2,1)} %tile.2), calls=%async_computation | async-start | bytes 8388608 | tf_op jit(solution)/shard_map/all_to_all | solution.py:17
  24.4 387.5 %all-gather.5.cloned.1.call-start = ((), (), s32[]{:S(2)}) async-start(), calls=%async_computation.2 | async-start | bytes 10485760 | tf_op jit(solution)/shard_map/all_gather | solution.py:23
  143.4 3.2 copy-start
  168.0 3.2 copy-start
  192.6 3.2 copy-start
  217.1 3.2 copy-start
  241.7 3.2 copy-start
  266.2 3.2 copy-start
  290.8 3.2 copy-start
  315.4 3.2 copy-start
Sparse Core Ops, SparseCore 0:
  10.1 104.3 all-gather.2
  327.8 84.0 all-gather.4
